TPU v7x, 256 devices: a whole 4x4x8 slice. The times are simulated.
256 devices in a mesh: group: 16 (over x, z_lo), fsdp: 16 (over z_hi, y, core).
Axes of the slice: x: 4, y: 4, z: 8 (z_hi: 2, z_lo: 4; z = z_hi * 4 + z_lo), core: 2. Of those that a mesh axis runs over, the one named last changes fastest.
Arguments:
- activations: bfloat16 [2, 16, 6144, 2560], P(None, 'group', 'fsdp'), may hold values from -6 to 6
- out_grads: bfloat16 [2, 16, 6144, 2560], P(None, 'group', 'fsdp'), may hold values from -0.078125 to 0.078125
- weight: bfloat16 [16, 2560, 2560], P('group', 'fsdp'), may hold values from -0.1 to 0.1
- first_moment: bfloat16 [16, 2560, 2560], P('group', 'fsdp'), may hold values from -0.2 to 0.2
- second_moment: bfloat16 [16, 2560, 2560], P('group', 'fsdp'), may hold values from 0.049804688 to 2
- step_index: int32 [1], replicated, may hold values from 0 to 63
Outputs:
- new_weight: bfloat16 [16, 2560, 2560], P('group', 'fsdp')
- new_moment: float32 [16, 2560, 2560], P('group', 'fsdp')
All inputs are finite; a program needn't handle non-finite values.
Results may differ from a plain program's by a relative error of at most 0.018.
Values may be sent and summed in bfloat16 or wider, within the bound.
No kernel may reach another device: no remote copies, remote signals or barrier semaphores. Data moves between devices by JAX's collectives and lax.ppermute only.
A program may use at most 192 MiB of HBM per device.

v0:
```python
from functools import partial

import jax
import jax.numpy as jnp
from jax import lax
from jax.experimental import pallas as pl
from jax.experimental.pallas import tpu as pltpu
from jax.sharding import PartitionSpec as P

LEARN_RATE = 0.05
WEIGHT_DECAY = 0.1
BETA_ONE = 0.9
BETA_TWO = 0.95
EPSILON = 1e-08

Z_HI, Y, CORES = 2, 4, 2
N_FSDP = Z_HI * Y * CORES
N_GROUP = 16
LEVELS = N_GROUP.bit_length() - 1
ROWS = 160
TOK = 384
WIDTH = 2560
CHUNKS = ((0, 1280), (1280, 1280))
TILE = 1280
STRIP = 16
SMALL = pl.CostEstimate(flops=1024, bytes_accessed=1024, transcendentals=0)
PARAMS = pltpu.CompilerParams(vmem_limit_bytes=32 * 1024 * 1024)


def held(array):
    return pltpu.with_memory_space_constraint(array, pltpu.HBM)


def fsdp_move(block, move):
    def target(i):
        z, y, c = i // (Y * CORES), (i // CORES) % Y, i % CORES
        z, y, c = move(z, y, c)
        return ((z % Z_HI) * Y + y % Y) * CORES + c % CORES

    return lax.ppermute(block, "fsdp", [(i, target(i)) for i in range(N_FSDP)])


def y_move(block, shift):
    return fsdp_move(block, lambda z, y, c: (z, y + shift, c))


def z_swap(block):
    return fsdp_move(block, lambda z, y, c: (z + 1, y, c))


def core_swap(block):
    return fsdp_move(block, lambda z, y, c: (z, y, c + 1))


def group_move(block, distance):
    return lax.ppermute(
        block, "group", [((i - distance) % N_GROUP, i) for i in range(N_GROUP)]
    )


def turn_kernel(core_ref, x_ref, *refs):
    own_ref, other_ref, turned = refs[-3:]

    def one(j, carry):
        at = pl.multiple_of(j * 256, 256)
        turned[pl.ds(at, 256), :] = x_ref[:, pl.ds(at, 256)].T
        return carry

    lax.fori_loop(0, WIDTH // 256, one, 0)
    core = core_ref[0]

    def give(b, carry):
        for ref, k in ((own_ref, core), (other_ref, 1 - core)):
            start = pl.multiple_of((b * CORES + k) * ROWS, ROWS)
            ref[b] = turned[pl.ds(start, ROWS), :]
        return carry

    lax.fori_loop(0, Z_HI * Y, give, 0)


def turn(core, x, step, after):
    shape = jax.ShapeDtypeStruct((Z_HI * Y, ROWS, TOK), jnp.bfloat16)
    return pl.pallas_call(
        turn_kernel,
        grid_spec=pltpu.PrefetchScalarGridSpec(
            num_scalar_prefetch=1,
            grid=(1,),
            in_specs=[pl.BlockSpec((None, None, TOK, WIDTH), lambda i, s: (step, 0, 0, 0))]
            + [pl.BlockSpec(memory_space=pl.ANY)] * len(after),
            out_specs=[pl.BlockSpec((Z_HI * Y, ROWS, TOK), lambda i, s: (0, 0, 0))] * 2,
            scratch_shapes=[pltpu.VMEM((WIDTH, TOK), jnp.bfloat16)],
        ),
        out_shape=[shape, shape],
        compiler_params=PARAMS,
        cost_estimate=SMALL,
    )(core, held(x), *after)


def products_kernel(adds, layout, terms, tiles, blocks_ref, *refs):
    units = len(adds)
    own, other = refs[:units], refs[units : 2 * units]
    at = 2 * units + 2 * tiles
    y_own, y_other = refs[2 * units : at - tiles], refs[at - tiles : at]
    given = [refs[at + t * tiles : at + (t + 1) * tiles] for t in range(terms)]
    outs = refs[len(refs) - len(layout) :]
    x = jnp.concatenate(
        [jnp.concatenate([a[0], b[0]], axis=1) for a, b in zip(own, other)], axis=0
    )
    total = jnp.concatenate(
        [
            jnp.dot(
                x,
                jnp.concatenate([a[...], b[...]], axis=0),
                preferred_element_type=jnp.float32,
            )
            for a, b in zip(y_own, y_other)
        ],
        axis=1,
    )
    parts = []
    for u, per_unit in enumerate(adds):
        part = total[u * ROWS : (u + 1) * ROWS]
        for term, plane in per_unit:
            more = jnp.concatenate([r[plane] for r in given[term]], axis=1)
            part = part + more.astype(jnp.float32)
        parts.append(part)
    for out, planes in zip(outs, layout):
        for p, u in enumerate(planes):
            out[p] = parts[u].astype(out.dtype)


def products(pair, step, chunk, blocks, adds, terms, layout, dtypes, after=(), hold=False):
    x_own, x_other, y_own, y_other = pair
    if hold:
        y_own, y_other = held(y_own), held(y_other)
    column, width = chunk
    units = len(adds)
    x_specs = [
        pl.BlockSpec((1, ROWS, TOK), lambda j, s, u=u: (s[u], 0, 0)) for u in range(units)
    ]
    tiles = width // TILE
    y_specs = [
        pl.BlockSpec((None, None, TOK, TILE), lambda j, s, t=t: (step, 0, 0, column // TILE + t))
        for t in range(tiles)
    ]

    t_specs = [
        pl.BlockSpec((t.shape[0], ROWS, TILE), lambda j, s, k=first // TILE + k: (0, 0, k))
        for t, first in terms
        for k in range(tiles)
    ]
    outs = [(len(planes), ROWS, width) for planes in layout]
    return pl.pallas_call(
        partial(products_kernel, adds, layout, len(terms), tiles),
        grid_spec=pltpu.PrefetchScalarGridSpec(
            num_scalar_prefetch=1,
            grid=(1,),
            in_specs=x_specs * 2
            + y_specs * 2
            + t_specs
            + [pl.BlockSpec(memory_space=pl.ANY)] * len(after),
            out_specs=[pl.BlockSpec(o, lambda j, s: (0, 0, 0)) for o in outs],
        ),
        out_shape=[jax.ShapeDtypeStruct(o, d) for o, d in zip(outs, dtypes)],
        compiler_params=PARAMS,
        cost_estimate=SMALL,
    )(
        blocks,
        *([x_own] * units),
        *([x_other] * units),
        *([y_own] * tiles),
        *([y_other] * tiles),
        *(t for t, _ in terms for _ in range(tiles)),
        *after,
    )


def strips(work):
    def one(i, carry):
        work(pl.ds(pl.multiple_of(i * STRIP, STRIP), STRIP))
        return carry

    lax.fori_loop(0, ROWS // STRIP, one, 0)


def by_columns(kernel, ins, outs, width, after=(), into=None):
    def spec(array, column, plane=0):
        lead = (None,) * (len(array.shape) - 2)
        return pl.BlockSpec(
            (*lead, ROWS, TILE), lambda j: (*(plane for _ in lead), 0, column // TILE + j)
        )

    shapes = [jax.ShapeDtypeStruct((ROWS, columns), dtype) for columns, _, dtype in outs]
    unread = list(after)
    aliases = {}
    if into is not None:
        aliases = {len(ins) + len(unread): len(outs) - 1}
        unread.append(into)

    def body(*refs):
        used = refs[: len(ins)] + refs[len(ins) + len(unread) :]
        strips(partial(kernel, *used))

    return pl.pallas_call(
        body,
        grid=(width // TILE,),
        in_specs=[spec(*i) for i in ins] + [pl.BlockSpec(memory_space=pl.ANY)] * len(unread),
        out_specs=[spec(shape, o[1]) for shape, o in zip(shapes, outs)],
        out_shape=shapes,
        input_output_aliases=aliases,
        compiler_params=PARAMS,
        cost_estimate=SMALL,
    )(*(i[0] for i in ins), *unread)


def adam(params, first, second, gradient):
    first = BETA_ONE * first + (1.0 - BETA_ONE) * gradient
    second = BETA_TWO * second + (1.0 - BETA_TWO) * gradient * gradient
    updated = params - LEARN_RATE * (first / (jnp.sqrt(second) + EPSILON) + WEIGHT_DECAY * params)
    return first, second, updated.astype(jnp.bfloat16)


def average(own, partner):
    return ((own.astype(jnp.float32) + partner.astype(jnp.float32)) * 0.5).astype(jnp.bfloat16)


def gradient_of(terms, at):
    total = terms[0][at].astype(jnp.float32)
    for term in terms[1:]:
        total = total + term[at].astype(jnp.float32)
    return total


def first_kernel(w, m, v, *rest):
    *terms, new_m, new_v, new_u, at = rest
    f32 = jnp.float32
    new_m[at], new_v[at], new_u[at] = adam(
        w[at].astype(f32), m[at].astype(f32), v[at].astype(f32), gradient_of(terms, at)
    )


def second_kernel(own, partner, m, v, *rest):
    *terms, new_u, new_m, at = rest
    w = average(own[at], partner[at]).astype(jnp.float32)
    new_m[at], _, new_u[at] = adam(w, m[at], v[at], gradient_of(terms, at))


def give_kernel(mine, mine_up, mine_down, other, up, down, total, give, at):
    total[at] = gradient_of((mine, mine_up, mine_down), at)
    give[at] = gradient_of((other, up, down), at).astype(give.dtype)


def average_kernel(own, partner, out, at):
    out[at] = average(own[at], partner[at])


def per_device(x, y, weight, first, second, step_index):
    index = lax.axis_index("fsdp")
    core, at_y, at_z = index % CORES, (index // CORES) % Y, index // (Y * CORES)
    bf16, f32 = jnp.bfloat16, jnp.float32

    def chosen(*pairs):
        rows = [((at_z + dz) % Z_HI) * Y + (at_y + dy) % Y for dy, dz in pairs]
        return jnp.stack(rows).astype(jnp.int32)

    core = core.astype(jnp.int32)[None]
    y_other = core_swap(y)
    last = []
    pairs = []
    for s in range(2):
        x_own, x_give = turn(core, x, s, tuple(last))
        last[:] = [x_own]
        pairs.append((x_own, core_swap(x_give), y, y_other))

    def go(step, chunk, blocks, adds, terms, layout, hold=False):
        outs = products(
            pairs[step],
            step,
            chunk,
            chosen(*blocks),
            adds,
            terms,
            layout,
            (bf16,) * len(layout),
            tuple(last),
            hold,
        )
        last[:] = [outs[0]]
        return outs

    def far(step, chunk):
        up, down = go(step, chunk, ((2, 0), (2, 1)), ((), ()), (), ((0,), (1,)), step == 0)
        return y_move(up, 1), y_move(down, -1)

    def near(step, chunk, arrived):
        up, down, mine, other = go(
            step,
            chunk,
            ((1, 0), (1, 1), (-1, 0), (-1, 1), (0, 0), (0, 1)),
            (((0, 0),), (), (), ((1, 0),), (), ()),
            [(t, chunk[0]) for t in arrived],
            ((0, 1), (2, 3), (4,), (5,)),
        )
        return y_move(up, 1), y_move(down, -1), mine, other

    def follow(kernel, ins, outs, width, into=None):
        results = by_columns(kernel, ins, outs, width, tuple(last), into)
        last[:] = [results[0]]
        return results

    def across(chunk, sums):
        up, down, mine, other = sums
        return follow(
            give_kernel,
            [(mine, 0), (up, 0), (down, 0), (other, 0), (up, 0, 1), (down, 0, 1)],
            [(chunk[1], 0, f32), (chunk[1], 0, bf16)],
            chunk[1],
        )

    def first_step(chunk, total, give):
        column, width = chunk
        return follow(
            first_kernel,
            [(t, column) for t in (weight, first, second)] + [(total, 0), (z_swap(give), 0)],
            [(width, 0, f32), (width, 0, f32), (width, 0, bf16)],
            width,
        )

    a, b = CHUNKS
    far_ab = far(0, (0, WIDTH))
    near_a = near(0, a, far_ab)
    far_cd = far(1, (0, WIDTH))
    sums_a = across(a, near_a)
    near_b = near(0, b, far_ab)
    near_c = near(1, a, far_cd)
    sums_b = across(b, near_b)
    state_a = first_step(a, *sums_a)
    near_d = near(1, b, far_cd)
    total_c, give_c = across(a, near_c)
    state_b = first_step(b, *sums_b)
    total_d, give_d = across(b, near_d)
    return lax.switch(
        step_index[0] % LEVELS,
        [partial(ending, level) for level in range(LEVELS)],
        state_a,
        state_b,
        total_c,
        total_d,
        z_swap(give_c),
        give_d,
    )


def ending(level, state_a, state_b, total_c, total_d, got_c, give_d):
    distances = 1 << level, 1 << ((level + 1) % LEVELS)
    bf16, f32 = jnp.bfloat16, jnp.float32
    partners = [group_move(state[2], distances[0]) for state in (state_a, state_b)]
    gots = got_c, z_swap(give_d)
    moments, after, boths = None, (), []
    for chunk, state, partner, total, got in zip(
        CHUNKS, (state_a, state_b), partners, (total_c, total_d), gots
    ):
        column, width = chunk
        m, v, u = state
        u, moments = by_columns(
            second_kernel,
            [(t, 0) for t in (u, partner, m, v, total, got)],
            [(width, 0, bf16), (WIDTH, column, f32)],
            width,
            after,
            moments,
        )
        after = (u,)
        boths.append((u, group_move(u, distances[1])))
    weights = None
    for (column, width), both in zip(CHUNKS, boths):
        (weights,) = by_columns(
            average_kernel, [(t, 0) for t in both], [(WIDTH, column, bf16)], width, after, weights
        )
        after = ()
    return weights[None], moments[None]


def solution(mesh):
    in_specs = (
        P(None, "group", "fsdp", None),
        P(None, "group", "fsdp", None),
        P("group", "fsdp", None),
        P("group", "fsdp", None),
        P("group", "fsdp", None),
        P(),
    )
    out_specs = (P("group", "fsdp", None), P("group", "fsdp", None))
    return jax.shard_map(
        per_device, mesh=mesh, in_specs=in_specs, out_specs=out_specs, check_vma=False
    )
```

profile of v0, /device:TPU:68, one launch (start us, length us, event | category | flops | bytes accessed | tf_op | source)
XLA Modules:
  0.0 195.0 jit_solution(4021582938159190795)
XLA Ops:
  0.7 3.8 %shard_map.85 = (bf16[8,160,384]{2,1,0:T(8,128)(2,1)S(1)}, bf16[8,160,384]{2,1,0:T(8,128)(2,1)}) custom-call(s32[1]{0:T(128)} %bitcast.15.core_ref, bf16[2,1,384,2560]{3,2,1,0:T(8,128)(2,1)} %x_ref.3), custom_call_target="tpu_custom_call" | custom-call | flops 1024 | bytes 1024 | tf_op jit(solution)/shard_map/pallas_call | solution.py:83
  4.5 0.5 collective-permute-start.20
  5.0 3.8 %shard_map.86 = (bf16[8,160,384]{2,1,0:T(8,128)(2,1)S(1)}, bf16[8,160,384]{2,1,0:T(8,128)(2,1)}) custom-call(s32[1]{0:T(128)} %bitcast.15.core_ref, bf16[2,1,384,2560]{3,2,1,0:T(8,128)(2,1)} %x_ref.3, bf16[8,160,384]{2,1,0:T(8,128)(2,1)S(1)} %get-tuple-element.176.refs_0_.refs_1_.refs_2_.refs_3_.refs_4_.refs_5_), custom_call_target="tpu_custom_call" | custom-call | flops 1024 | bytes 1024 | tf_op jit(solution)/shard_map/pallas_call | solution.py:83
  9.1 5.2 %shard_map.87 = (bf16[1,160,2560]{2,1,0:T(8,128)(2,1)}, bf16[1,160,2560]{2,1,0:T(8,128)(2,1)}) custom-call(s32[2]{0:T(128)S(1)} %pad_add_fusion.blocks_ref, bf16[8,160,384]{2,1,0:T(8,128)(2,1)S(1)} %get-tuple-element.176.refs_0_.refs_1_.refs_2_.refs_3_.refs_4_.refs_5_, ...), custom_call_target="tpu_custom_call" | custom-call | flops 1024 | bytes 1024 | tf_op jit(solution)/shard_map/pallas_call | solution.py:153
  14.3 1.6 collective-permute-start.22
  15.9 1.6 collective-permute-start.23
  17.6 18.6 %collective-permute-done.22.refs_14_ = bf16[1,160,2560]{2,1,0:T(8,128)(2,1)} collective-permute-done((bf16[1,160,2560]{2,1,0:T(8,128)(2,1)}, bf16[1,160,2560]{2,1,0:T(8,128)(2,1)}, u32[]{:S(2)}, u32[]{:S(2)}) %collective-permute-start.22) | collective-permute-done | bytes 819232 | tf_op jit(solution)/shard_map/ppermute | solution.py:40
  36.2 2.1 %copy-done = bf16[2,1,384,2560]{3,2,1,0:T(8,128)(2,1)S(1)} copy-done((bf16[2,1,384,2560]{3,2,1,0:T(8,128)(2,1)S(1)}, bf16[2,1,384,2560]{3,2,1,0:T(8,128)(2,1)}, u32[]{:S(2)}) %copy-start) | copy-done | bytes 3932184
  38.4 4.3 %shard_map.88 = (bf16[2,160,1280]{2,1,0:T(8,128)(2,1)S(1)}, bf16[2,160,1280]{2,1,0:T(8,128)(2,1)S(1)}, bf16[1,160,1280]{2,1,0:T(8,128)(2,1)S(1)}, bf16[1,160,1280]{2,1,0:T(8,128)(2,1)S(1)}) custom-call(s32[6]{0:T(128)S(1)} %stack.26.blocks_ref, bf16[8,160,384]{2,1,0:T(8,128)(2,1)S(1)} %get-tuple-element.176.refs_0_.refs_1_.refs_2_.refs_3_.refs_4_.refs_5_, ...), custom_call_target="tpu_custom_call" | custom-call | flops 1024 | bytes 1024 | tf_op jit(solution)/shard_map/pallas_call | solution.py:153
  42.7 1.6 collective-permute-start.24
  44.3 1.7 collective-permute-start.25
  46.0 3.6 %shard_map.89 = (bf16[1,160,2560]{2,1,0:T(8,128)(2,1)S(1)}, bf16[1,160,2560]{2,1,0:T(8,128)(2,1)S(1)}) custom-call(s32[2]{0:T(128)S(1)} %pad_add_fusion.blocks_ref, bf16[8,160,384]{2,1,0:T(8,128)(2,1)S(1)} %get-tuple-element.178.refs_8_.refs_0_.refs_1_.refs_2_.refs_3_.refs_4_.refs_5_, ...), custom_call_target="tpu_custom_call" | custom-call | flops 1024 | bytes 1024 | tf_op jit(solution)/shard_map/pallas_call | solution.py:153
  50.1 2.9 %collective-permute-start.30 = (bf16[1,160,2560]{2,1,0:T(8,128)(2,1)S(1)}, bf16[1,160,2560]{2,1,0:T(8,128)(2,1)S(1)}, u32[]{:S(2)}, u32[]{:S(2)}) collective-permute-start(bf16[1,160,2560]{2,1,0:T(8,128)(2,1)S(1)} %get-tuple-element.192), channel_id=1, source_target_pairs={{0,6},{1,7},{2,0},{3,1},{4,2},{5,3},{6,4},{7,5},{8,14},{9,15},{10,... | collective-permute-start | bytes 2457608 | tf_op jit(solution)/shard_map/ppermute | solution.py:40
  53.0 12.2 %collective-permute-done.24.refs_1_.refs_4_ = bf16[2,160,1280]{2,1,0:T(8,128)(2,1)S(1)} collective-permute-done((bf16[2,160,1280]{2,1,0:T(8,128)(2,1)S(1)}, bf16[2,160,1280]{2,1,0:T(8,128)(2,1)S(1)}, u32[]{:S(2)}, u32[]{:S(2)}) %collective-permute-start.24) | collective-permute-done | bytes 819232 | tf_op jit(solution)/shard_map/ppermute | solution.py:40
  65.8 4.1 %shard_map.91 = (bf16[2,160,1280]{2,1,0:T(8,128)(2,1)S(1)}, bf16[2,160,1280]{2,1,0:T(8,128)(2,1)S(1)}, bf16[1,160,1280]{2,1,0:T(8,128)(2,1)S(1)}, bf16[1,160,1280]{2,1,0:T(8,128)(2,1)S(1)}) custom-call(s32[6]{0:T(128)S(1)} %stack.26.blocks_ref, bf16[8,160,384]{2,1,0:T(8,128)(2,1)S(1)} %get-tuple-element.176.refs_0_.refs_1_.refs_2_.refs_3_.refs_4_.refs_5_, ...), custom_call_target="tpu_custom_call" | custom-call | flops 1024 | bytes 1024 | tf_op jit(solution)/shard_map/pallas_call | solution.py:153
  69.9 1.6 collective-permute-start.27
  71.5 1.9 collective-permute-start.28
  73.4 5.4 %collective-permute-start.34 = (bf16[160,1280]{1,0:T(8,128)(2,1)S(1)}, bf16[160,1280]{1,0:T(8,128)(2,1)S(1)}, u32[]{:S(2)}, u32[]{:S(2)}) collective-permute-start(bf16[160,1280]{1,0:T(8,128)(2,1)S(1)} %get-tuple-element.199), channel_id=1, source_target_pairs={{0,8},{1,9},{2,10},{3,11},{4,12},{5,13},{6,14},{7,15},{8,0},{9,1},... | collective-permute-start | bytes 1228808 | tf_op jit(solution)/shard_map/ppermute | solution.py:40
  78.8 3.9 %collective-permute-done.29.refs_14_ = bf16[1,160,2560]{2,1,0:T(8,128)(2,1)S(1)} collective-permute-done((bf16[1,160,2560]{2,1,0:T(8,128)(2,1)S(1)}, bf16[1,160,2560]{2,1,0:T(8,128)(2,1)S(1)}, u32[]{:S(2)}, u32[]{:S(2)}) %collective-permute-start.29) | collective-permute-done | bytes 819232 | tf_op jit(solution)/shard_map/ppermute | solution.py:40
  83.0 4.2 %shard_map.92 = (bf16[2,160,1280]{2,1,0:T(8,128)(2,1)S(1)}, bf16[2,160,1280]{2,1,0:T(8,128)(2,1)S(1)}, bf16[1,160,1280]{2,1,0:T(8,128)(2,1)S(1)}, bf16[1,160,1280]{2,1,0:T(8,128)(2,1)S(1)}) custom-call(s32[6]{0:T(128)S(1)} %stack.26.blocks_ref, bf16[8,160,384]{2,1,0:T(8,128)(2,1)S(1)} %get-tuple-element.178.refs_8_.refs_0_.refs_1_.refs_2_.refs_3_.refs_4_.refs_5_, ...), custom_call_target="tpu_custom_call" | custom-call | flops 1024 | bytes 1024 | tf_op jit(solution)/shard_map/pallas_call | solution.py:153
  87.2 1.4 collective-permute-start.32
  88.6 1.9 collective-permute-start.33
  90.6 9.7 %collective-permute-done.27.refs_1_.refs_4_ = bf16[2,160,1280]{2,1,0:T(8,128)(2,1)S(1)} collective-permute-done((bf16[2,160,1280]{2,1,0:T(8,128)(2,1)S(1)}, bf16[2,160,1280]{2,1,0:T(8,128)(2,1)S(1)}, u32[]{:S(2)}, u32[]{:S(2)}) %collective-permute-start.27) | collective-permute-done | bytes 819232 | tf_op jit(solution)/shard_map/ppermute | solution.py:40
  100.6 1.1 shard_map.93
  102.4 2.0 %shard_map.94 = (f32[160,1280]{1,0:T(8,128)S(1)}, f32[160,1280]{1,0:T(8,128)}, bf16[160,1280]{1,0:T(8,128)(2,1)}) custom-call(bf16[1,160,2560]{2,1,0:T(8,128)(2,1)S(1)} %copy-done.2, bf16[1,160,2560]{2,1,0:T(8,128)(2,1)S(1)} %copy-done.3, bf16[1,160,2560]{2,1,0:T(8,128)(2,1)S(1)} %copy-done.4, f32[160,1280]{1,0:T(8,128)S(1)} %get-tuple-element.187.refs_16_.refs_3_, ...), custom_call_target="tpu_custom_call" | custom-call | flops 1024 | bytes 1024 | tf_op jit(solution)/shard_map/pallas_call | solution.py:204
  104.4 5.3 %shard_map.95 = (bf16[2,160,1280]{2,1,0:T(8,128)(2,1)}, bf16[2,160,1280]{2,1,0:T(8,128)(2,1)}, bf16[1,160,1280]{2,1,0:T(8,128)(2,1)S(1)}, bf16[1,160,1280]{2,1,0:T(8,128)(2,1)S(1)}) custom-call(s32[6]{0:T(128)S(1)} %stack.26.blocks_ref, bf16[8,160,384]{2,1,0:T(8,128)(2,1)S(1)} %get-tuple-element.178.refs_8_.refs_0_.refs_1_.refs_2_.refs_3_.refs_4_.refs_5_, ...), custom_call_target="tpu_custom_call" | custom-call | flops 1024 | bytes 1024 | tf_op jit(solution)/shard_map/pallas_call | solution.py:153
  109.7 1.4 collective-permute-start.35
  111.1 1.9 collective-permute-start.36
  113.0 5.4 %collective-permute-start.31 = (bf16[160,1280]{1,0:T(8,128)(2,1)}, bf16[160,1280]{1,0:T(8,128)(2,1)}, u32[]{:S(2)}, u32[]{:S(2)}) collective-permute-start(bf16[160,1280]{1,0:T(8,128)(2,1)} %get-tuple-element.195), channel_id=1, source_target_pairs={{0,8},{1,9},{2,10},{3,11},{4,12},{5,13},{6,14},{7,15},{8,0},{9,1},... | collective-permute-start | bytes 1228808 | tf_op jit(solution)/shard_map/ppermute | solution.py:40
  118.4 1.3 shard_map.96
  119.7 5.2 %collective-permute-start.37 = (bf16[160,1280]{1,0:T(8,128)(2,1)}, bf16[160,1280]{1,0:T(8,128)(2,1)}, u32[]{:S(2)}, u32[]{:S(2)}) collective-permute-start(bf16[160,1280]{1,0:T(8,128)(2,1)} %get-tuple-element.211), channel_id=1, source_target_pairs={{0,8},{1,9},{2,10},{3,11},{4,12},{5,13},{6,14},{7,15},{8,0},{9,1},... | collective-permute-start | bytes 1228808 | tf_op jit(solution)/shard_map/ppermute | solution.py:40
  125.6 17.5 %collective-permute-done.31.refs_4_ = bf16[160,1280]{1,0:T(8,128)(2,1)} collective-permute-done((bf16[160,1280]{1,0:T(8,128)(2,1)}, bf16[160,1280]{1,0:T(8,128)(2,1)}, u32[]{:S(2)}, u32[]{:S(2)}) %collective-permute-start.31) | collective-permute-done | bytes 409632 | tf_op jit(solution)/shard_map/ppermute | solution.py:40
  143.0 1.1 copy-done.5
  144.2 1.1 copy-done.7
  145.3 2.0 %shard_map.97 = (f32[160,1280]{1,0:T(8,128)S(1)}, f32[160,1280]{1,0:T(8,128)S(1)}, bf16[160,1280]{1,0:T(8,128)(2,1)S(1)}) custom-call(bf16[1,160,2560]{2,1,0:T(8,128)(2,1)S(1)} %copy-done.2, bf16[1,160,2560]{2,1,0:T(8,128)(2,1)S(1)} %copy-done.3, bf16[1,160,2560]{2,1,0:T(8,128)(2,1)S(1)} %copy-done.5, f32[160,1280]{1,0:T(8,128)S(1)} %copy-done.7, ...), custom_call_target="tpu_custom_call" | custom-call | flops 1024 | bytes 1024 | tf_op jit(solution)/shard_map/pallas_call | solution.py:204
  147.7 3.3 %collective-permute-done.37 = bf16[160,1280]{1,0:T(8,128)(2,1)} collective-permute-done((bf16[160,1280]{1,0:T(8,128)(2,1)}, bf16[160,1280]{1,0:T(8,128)(2,1)}, u32[]{:S(2)}, u32[]{:S(2)}) %collective-permute-start.37) | collective-permute-done | bytes 409632 | tf_op jit(solution)/shard_map/ppermute | solution.py:40
  151.1 43.9 %conditional.1 = (bf16[1,160,2560]{2,1,0:T(8,128)(2,1)}, f32[1,160,2560]{2,1,0:T(8,128)}) conditional(s32[]{:T(128)} %clamp.3, (bf16[160,1280]{1,0:T(8,128)(2,1)S(1)}, bf16[160,1280]{1,0:T(8,128)(2,1)S(1)}, bf16[160,1280]{1,0:T(8,128)(2,1)S(1)}, f32[160,1280]{1,0:T(8,128)S(1)}, f32[160,1280]{1,0:T(8,128)S(1)}, ...), branch_computations={%region_0.1_spmd, %region_1.2_spmd, %region_2.3_spmd, %region_3.4_... | conditional | flops 4096 | bytes 18026768 | solution.py:342
  151.3 0.6 collective-permute-start.17
  151.9 3.0 %collective-permute-start.15 = (bf16[160,1280]{1,0:T(8,128)(2,1)S(1)}, bf16[160,1280]{1,0:T(8,128)(2,1)S(1)}, u32[]{:S(2)}, u32[]{:S(2)}) collective-permute-start(bf16[160,1280]{1,0:T(8,128)(2,1)S(1)} %get-tuple-element.122.refs_0_), channel_id=1, source_target_pairs={{128,0},{144,16},{160,32},{176,48},{192,64},{208,80},{224,96},{240... | collective-permute-start | bytes 1228808 | tf_op jit(solution)/shard_map/cond/branch_3_fun/ppermute | solution.py:56
  155.0 5.1 %collective-permute-start.16 = (bf16[160,1280]{1,0:T(8,128)(2,1)S(1)}, bf16[160,1280]{1,0:T(8,128)(2,1)S(1)}, u32[]{:S(2)}, u32[]{:S(2)}) collective-permute-start(bf16[160,1280]{1,0:T(8,128)(2,1)S(1)} %get-tuple-element.126), channel_id=1, source_target_pairs={{0,8},{1,9},{2,10},{3,11},{4,12},{5,13},{6,14},{7,15},{8,0},{9,1},... | collective-permute-start | bytes 1228808 | tf_op jit(solution)/shard_map/cond/branch_3_fun/ppermute | solution.py:40
  160.1 5.3 %collective-permute-done.17.refs_1_ = bf16[160,1280]{1,0:T(8,128)(2,1)S(1)} collective-permute-done((bf16[160,1280]{1,0:T(8,128)(2,1)S(1)}, bf16[160,1280]{1,0:T(8,128)(2,1)S(1)}, u32[]{:S(2)}, u32[]{:S(2)}) %collective-permute-start.17) | collective-permute-done | bytes 409632 | tf_op jit(solution)/shard_map/cond/branch_3_fun/ppermute | solution.py:56
  165.3 1.9 branch_3_fun.4
  167.4 4.9 %collective-permute-done.15.refs_1_ = bf16[160,1280]{1,0:T(8,128)(2,1)S(1)} collective-permute-done((bf16[160,1280]{1,0:T(8,128)(2,1)S(1)}, bf16[160,1280]{1,0:T(8,128)(2,1)S(1)}, u32[]{:S(2)}, u32[]{:S(2)}) %collective-permute-start.15) | collective-permute-done | bytes 409632 | tf_op jit(solution)/shard_map/cond/branch_3_fun/ppermute | solution.py:56
  172.3 2.7 %collective-permute-done.16.refs_5_ = bf16[160,1280]{1,0:T(8,128)(2,1)S(1)} collective-permute-done((bf16[160,1280]{1,0:T(8,128)(2,1)S(1)}, bf16[160,1280]{1,0:T(8,128)(2,1)S(1)}, u32[]{:S(2)}, u32[]{:S(2)}) %collective-permute-start.16) | collective-permute-done | bytes 409632 | tf_op jit(solution)/shard_map/cond/branch_3_fun/ppermute | solution.py:40
  175.0 0.9 branch_3_fun.5
  176.1 8.7 %collective-permute-done.19.refs_1_ = bf16[160,1280]{1,0:T(8,128)(2,1)S(1)} collective-permute-done((bf16[160,1280]{1,0:T(8,128)(2,1)S(1)}, bf16[160,1280]{1,0:T(8,128)(2,1)S(1)}, u32[]{:S(2)}, u32[]{:S(2)}) %collective-permute-start.19) | collective-permute-done | bytes 409632 | tf_op jit(solution)/shard_map/cond/branch_3_fun/ppermute | solution.py:56
  185.0 8.9 %collective-permute-done.18.refs_1_ = bf16[160,1280]{1,0:T(8,128)(2,1)S(1)} collective-permute-done((bf16[160,1280]{1,0:T(8,128)(2,1)S(1)}, bf16[160,1280]{1,0:T(8,128)(2,1)S(1)}, u32[]{:S(2)}, u32[]{:S(2)}) %collective-permute-start.18) | collective-permute-done | bytes 409632 | tf_op jit(solution)/shard_map/cond/branch_3_fun/ppermute | solution.py:56
  194.1 0.9 copy-done.22
  (57 shorter events, 3.9 us)
Async XLA Ops:
  0.6 8.5 %collective-permute-start.21 = (bf16[2,1,384,2560]{3,2,1,0:T(8,128)(2,1)}, bf16[2,1,384,2560]{3,2,1,0:T(8,128)(2,1)}, u32[]{:S(2)}, u32[]{:S(2)}) collective-permute-start(bf16[2,1,384,2560]{3,2,1,0:T(8,128)(2,1)} %refs_12_.7), channel_id=1, source_target_pairs={{0,1},{1,0},{2,3},{3,2},{4,5},{5,4},{6,7},{7,6},{8,9},{9,8},{10,11... | collective-permute-start | bytes 11796488 | tf_op jit(solution)/shard_map/ppermute | solution.py:40
  4.5 4.6 %collective-permute-start.20 = (bf16[8,160,384]{2,1,0:T(8,128)(2,1)}, bf16[8,160,384]{2,1,0:T(8,128)(2,1)S(1)}, u32[]{:S(2)}, u32[]{:S(2)}) collective-permute-start(bf16[8,160,384]{2,1,0:T(8,128)(2,1)} %get-tuple-element.177), channel_id=1, source_target_pairs={{0,1},{1,0},{2,3},{3,2},{4,5},{5,4},{6,7},{7,6},{8,9},{9,8},{10,11... | collective-permute-start | bytes 2949128 | tf_op jit(solution)/shard_map/ppermute | solution.py:40
  14.3 21.9 %collective-permute-start.22 = (bf16[1,160,2560]{2,1,0:T(8,128)(2,1)}, bf16[1,160,2560]{2,1,0:T(8,128)(2,1)}, u32[]{:S(2)}, u32[]{:S(2)}) collective-permute-start(bf16[1,160,2560]{2,1,0:T(8,128)(2,1)} %get-tuple-element.179.refs_16_), channel_id=1, source_target_pairs={{0,2},{1,3},{2,4},{3,5},{4,6},{5,7},{6,0},{7,1},{8,10},{9,11},{10,... | collective-permute-start | bytes 2457608 | tf_op jit(solution)/shard_map/ppermute | solution.py:40
  15.9 20.3 %collective-permute-start.23 = (bf16[1,160,2560]{2,1,0:T(8,128)(2,1)}, bf16[1,160,2560]{2,1,0:T(8,128)(2,1)}, u32[]{:S(2)}, u32[]{:S(2)}) collective-permute-start(bf16[1,160,2560]{2,1,0:T(8,128)(2,1)} %get-tuple-element.180), channel_id=1, source_target_pairs={{0,6},{1,7},{2,0},{3,1},{4,2},{5,3},{6,4},{7,5},{8,14},{9,15},{10,... | collective-permute-start | bytes 2457608 | tf_op jit(solution)/shard_map/ppermute | solution.py:40
  17.5 28.5 %collective-permute-start.26 = (bf16[8,160,384]{2,1,0:T(8,128)(2,1)}, bf16[8,160,384]{2,1,0:T(8,128)(2,1)}, u32[]{:S(2)}, u32[]{:S(2)}) collective-permute-start(bf16[8,160,384]{2,1,0:T(8,128)(2,1)} %get-tuple-element.185), channel_id=1, source_target_pairs={{0,1},{1,0},{2,3},{3,2},{4,5},{5,4},{6,7},{7,6},{8,9},{9,8},{10,11... | collective-permute-start | bytes 2949128 | tf_op jit(solution)/shard_map/ppermute | solution.py:40
  36.2 2.1 %copy-start = (bf16[2,1,384,2560]{3,2,1,0:T(8,128)(2,1)S(1)}, bf16[2,1,384,2560]{3,2,1,0:T(8,128)(2,1)}, u32[]{:S(2)}) copy-start(bf16[2,1,384,2560]{3,2,1,0:T(8,128)(2,1)} %refs_12_.7) | copy-start | bytes 11796484
  38.4 7.7 %copy-start.1 = (bf16[2,1,384,2560]{3,2,1,0:T(8,128)(2,1)S(1)}, bf16[2,1,384,2560]{3,2,1,0:T(8,128)(2,1)}, u32[]{:S(2)}) copy-start(bf16[2,1,384,2560]{3,2,1,0:T(8,128)(2,1)} %refs_12_.7) | copy-start | bytes 11796484
  42.7 22.5 %collective-permute-start.24 = (bf16[2,160,1280]{2,1,0:T(8,128)(2,1)S(1)}, bf16[2,160,1280]{2,1,0:T(8,128)(2,1)S(1)}, u32[]{:S(2)}, u32[]{:S(2)}) collective-permute-start(bf16[2,160,1280]{2,1,0:T(8,128)(2,1)S(1)} %get-tuple-element.182.refs_8_), channel_id=1, source_target_pairs={{0,2},{1,3},{2,4},{3,5},{4,6},{5,7},{6,0},{7,1},{8,10},{9,11},{10,... | collective-permute-start | bytes 2457608 | tf_op jit(solution)/shard_map/ppermute | solution.py:40
  44.3 21.2 %collective-permute-start.25 = (bf16[2,160,1280]{2,1,0:T(8,128)(2,1)S(1)}, bf16[2,160,1280]{2,1,0:T(8,128)(2,1)S(1)}, u32[]{:S(2)}, u32[]{:S(2)}) collective-permute-start(bf16[2,160,1280]{2,1,0:T(8,128)(2,1)S(1)} %get-tuple-element.183), channel_id=1, source_target_pairs={{0,6},{1,7},{2,0},{3,1},{4,2},{5,3},{6,4},{7,5},{8,14},{9,15},{10,... | collective-permute-start | bytes 2457608 | tf_op jit(solution)/shard_map/ppermute | solution.py:40
  49.6 33.1 %collective-permute-start.29 = (bf16[1,160,2560]{2,1,0:T(8,128)(2,1)S(1)}, bf16[1,160,2560]{2,1,0:T(8,128)(2,1)S(1)}, u32[]{:S(2)}, u32[]{:S(2)}) collective-permute-start(bf16[1,160,2560]{2,1,0:T(8,128)(2,1)S(1)} %get-tuple-element.186.refs_6_), channel_id=1, source_target_pairs={{0,2},{1,3},{2,4},{3,5},{4,6},{5,7},{6,0},{7,1},{8,10},{9,11},{10,... | collective-permute-start | bytes 2457608 | tf_op jit(solution)/shard_map/ppermute | solution.py:40
  50.1 33.0 %collective-permute-start.30 = (bf16[1,160,2560]{2,1,0:T(8,128)(2,1)S(1)}, bf16[1,160,2560]{2,1,0:T(8,128)(2,1)S(1)}, u32[]{:S(2)}, u32[]{:S(2)}) collective-permute-start(bf16[1,160,2560]{2,1,0:T(8,128)(2,1)S(1)} %get-tuple-element.192), channel_id=1, source_target_pairs={{0,6},{1,7},{2,0},{3,1},{4,2},{5,3},{6,4},{7,5},{8,14},{9,15},{10,... | collective-permute-start | bytes 2457608 | tf_op jit(solution)/shard_map/ppermute | solution.py:40
  69.9 30.4 %collective-permute-start.27 = (bf16[2,160,1280]{2,1,0:T(8,128)(2,1)S(1)}, bf16[2,160,1280]{2,1,0:T(8,128)(2,1)S(1)}, u32[]{:S(2)}, u32[]{:S(2)}) collective-permute-start(bf16[2,160,1280]{2,1,0:T(8,128)(2,1)S(1)} %get-tuple-element.189.refs_16_), channel_id=1, source_target_pairs={{0,2},{1,3},{2,4},{3,5},{4,6},{5,7},{6,0},{7,1},{8,10},{9,11},{10,... | collective-permute-start | bytes 2457608 | tf_op jit(solution)/shard_map/ppermute | solution.py:40
  71.5 29.1 %collective-permute-start.28 = (bf16[2,160,1280]{2,1,0:T(8,128)(2,1)S(1)}, bf16[2,160,1280]{2,1,0:T(8,128)(2,1)S(1)}, u32[]{:S(2)}, u32[]{:S(2)}) collective-permute-start(bf16[2,160,1280]{2,1,0:T(8,128)(2,1)S(1)} %get-tuple-element.190), channel_id=1, source_target_pairs={{0,6},{1,7},{2,0},{3,1},{4,2},{5,3},{6,4},{7,5},{8,14},{9,15},{10,... | collective-permute-start | bytes 2457608 | tf_op jit(solution)/shard_map/ppermute | solution.py:40
  73.4 28.3 %collective-permute-start.34 = (bf16[160,1280]{1,0:T(8,128)(2,1)S(1)}, bf16[160,1280]{1,0:T(8,128)(2,1)S(1)}, u32[]{:S(2)}, u32[]{:S(2)}) collective-permute-start(bf16[160,1280]{1,0:T(8,128)(2,1)S(1)} %get-tuple-element.199), channel_id=1, source_target_pairs={{0,8},{1,9},{2,10},{3,11},{4,12},{5,13},{6,14},{7,15},{8,0},{9,1},... | collective-permute-start | bytes 1228808 | tf_op jit(solution)/shard_map/ppermute | solution.py:40
  87.2 31.1 %collective-permute-start.32 = (bf16[2,160,1280]{2,1,0:T(8,128)(2,1)S(1)}, bf16[2,160,1280]{2,1,0:T(8,128)(2,1)S(1)}, u32[]{:S(2)}, u32[]{:S(2)}) collective-permute-start(bf16[2,160,1280]{2,1,0:T(8,128)(2,1)S(1)} %get-tuple-element.193.refs_6_), channel_id=1, source_target_pairs={{0,2},{1,3},{2,4},{3,5},{4,6},{5,7},{6,0},{7,1},{8,10},{9,11},{10,... | collective-permute-start | bytes 2457608 | tf_op jit(solution)/shard_map/ppermute | solution.py:40
  88.6 29.7 %collective-permute-start.33 = (bf16[2,160,1280]{2,1,0:T(8,128)(2,1)S(1)}, bf16[2,160,1280]{2,1,0:T(8,128)(2,1)S(1)}, u32[]{:S(2)}, u32[]{:S(2)}) collective-permute-start(bf16[2,160,1280]{2,1,0:T(8,128)(2,1)S(1)} %get-tuple-element.197), channel_id=1, source_target_pairs={{0,6},{1,7},{2,0},{3,1},{4,2},{5,3},{6,4},{7,5},{8,14},{9,15},{10,... | collective-permute-start | bytes 2457608 | tf_op jit(solution)/shard_map/ppermute | solution.py:40
  100.6 1.1 copy-start.2
  100.6 1.5 copy-start.3
  100.6 1.8 copy-start.4
  101.7 2.6 %copy-start.6 = (f32[160,1280]{1,0:T(8,128)}, f32[160,1280]{1,0:T(8,128)S(1)}, u32[]{:S(2)}) copy-start(f32[160,1280]{1,0:T(8,128)S(1)} %get-tuple-element.194.refs_5_.refs_3_) | copy-start | bytes 2457604
  104.3 5.3 %copy-start.17 = (f32[160,1280]{1,0:T(8,128)}, f32[160,1280]{1,0:T(8,128)S(1)}, u32[]{:S(2)}) copy-start(f32[160,1280]{1,0:T(8,128)S(1)} %get-tuple-element.200.refs_16_) | copy-start | bytes 2457604
  109.6 10.1 %copy-start.8 = (bf16[1,160,1280]{2,1,0:T(8,128)(2,1)}, bf16[1,160,1280]{2,1,0:T(8,128)(2,1)S(1)}, u32[]{:S(2)}) copy-start(bf16[1,160,1280]{2,1,0:T(8,128)(2,1)S(1)} %get-tuple-element.204.refs_0_) | copy-start | bytes 1228804
  109.6 10.1 %copy-start.10 = (bf16[1,160,1280]{2,1,0:T(8,128)(2,1)}, bf16[1,160,1280]{2,1,0:T(8,128)(2,1)S(1)}, u32[]{:S(2)}) copy-start(bf16[1,160,1280]{2,1,0:T(8,128)(2,1)S(1)} %get-tuple-element.206.refs_3_) | copy-start | bytes 1228804
  109.7 37.6 %collective-permute-start.35 = (bf16[2,160,1280]{2,1,0:T(8,128)(2,1)}, bf16[2,160,1280]{2,1,0:T(8,128)(2,1)S(1)}, u32[]{:S(2)}, u32[]{:S(2)}) collective-permute-start(bf16[2,160,1280]{2,1,0:T(8,128)(2,1)} %get-tuple-element.201.refs_6_), channel_id=1, source_target_pairs={{0,2},{1,3},{2,4},{3,5},{4,6},{5,7},{6,0},{7,1},{8,10},{9,11},{10,... | collective-permute-start | bytes 2457608 | tf_op jit(solution)/shard_map/ppermute | solution.py:40
  111.1 36.3 %collective-permute-start.36 = (bf16[2,160,1280]{2,1,0:T(8,128)(2,1)}, bf16[2,160,1280]{2,1,0:T(8,128)(2,1)S(1)}, u32[]{:S(2)}, u32[]{:S(2)}) collective-permute-start(bf16[2,160,1280]{2,1,0:T(8,128)(2,1)} %get-tuple-element.205), channel_id=1, source_target_pairs={{0,6},{1,7},{2,0},{3,1},{4,2},{5,3},{6,4},{7,5},{8,14},{9,15},{10,... | collective-permute-start | bytes 2457608 | tf_op jit(solution)/shard_map/ppermute | solution.py:40
  113.0 30.1 %collective-permute-start.31 = (bf16[160,1280]{1,0:T(8,128)(2,1)}, bf16[160,1280]{1,0:T(8,128)(2,1)}, u32[]{:S(2)}, u32[]{:S(2)}) collective-permute-start(bf16[160,1280]{1,0:T(8,128)(2,1)} %get-tuple-element.195), channel_id=1, source_target_pairs={{0,8},{1,9},{2,10},{3,11},{4,12},{5,13},{6,14},{7,15},{8,0},{9,1},... | collective-permute-start | bytes 1228808 | tf_op jit(solution)/shard_map/ppermute | solution.py:40
  119.7 31.3 %collective-permute-start.37 = (bf16[160,1280]{1,0:T(8,128)(2,1)}, bf16[160,1280]{1,0:T(8,128)(2,1)}, u32[]{:S(2)}, u32[]{:S(2)}) collective-permute-start(bf16[160,1280]{1,0:T(8,128)(2,1)} %get-tuple-element.211), channel_id=1, source_target_pairs={{0,8},{1,9},{2,10},{3,11},{4,12},{5,13},{6,14},{7,15},{8,0},{9,1},... | collective-permute-start | bytes 1228808 | tf_op jit(solution)/shard_map/ppermute | solution.py:40
  143.0 1.1 copy-start.5
  144.2 1.1 copy-start.7
  145.3 2.0 %copy-start.9 = (bf16[1,160,1280]{2,1,0:T(8,128)(2,1)S(1)}, bf16[1,160,1280]{2,1,0:T(8,128)(2,1)}, u32[]{:S(2)}) copy-start(bf16[1,160,1280]{2,1,0:T(8,128)(2,1)} %copy-done.8) | copy-start | bytes 1228804
  145.3 2.0 %copy-start.11 = (bf16[1,160,1280]{2,1,0:T(8,128)(2,1)S(1)}, bf16[1,160,1280]{2,1,0:T(8,128)(2,1)}, u32[]{:S(2)}) copy-start(bf16[1,160,1280]{2,1,0:T(8,128)(2,1)} %copy-done.10) | copy-start | bytes 1228804
  147.3 3.7 %copy-start.16 = (f32[160,1280]{1,0:T(8,128)S(1)}, f32[160,1280]{1,0:T(8,128)}, u32[]{:S(2)}) copy-start(f32[160,1280]{1,0:T(8,128)} %get-tuple-element.202.refs_5_) | copy-start | bytes 2457604
  147.4 3.7 %copy-start.18 = (f32[160,1280]{1,0:T(8,128)S(1)}, f32[160,1280]{1,0:T(8,128)}, u32[]{:S(2)}) copy-start(f32[160,1280]{1,0:T(8,128)} %copy-done.17) | copy-start | bytes 2457604
  147.4 3.7 %copy-start.23 = (f32[160,1280]{1,0:T(8,128)S(1)}, f32[160,1280]{1,0:T(8,128)}, u32[]{:S(2)}) copy-start(f32[160,1280]{1,0:T(8,128)} %get-tuple-element.210) | copy-start | bytes 2457604
  147.4 3.7 %copy-start.24 = (bf16[160,1280]{1,0:T(8,128)(2,1)S(1)}, bf16[160,1280]{1,0:T(8,128)(2,1)}, u32[]{:S(2)}) copy-start(bf16[160,1280]{1,0:T(8,128)(2,1)} %get-tuple-element.209) | copy-start | bytes 1228804
  151.3 14.0 %collective-permute-start.17 = (bf16[160,1280]{1,0:T(8,128)(2,1)S(1)}, bf16[160,1280]{1,0:T(8,128)(2,1)S(1)}, u32[]{:S(2)}, u32[]{:S(2)}) collective-permute-start(bf16[160,1280]{1,0:T(8,128)(2,1)S(1)} %get-tuple-element.127.refs_0_), channel_id=1, source_target_pairs={{128,0},{144,16},{160,32},{176,48},{192,64},{208,80},{224,96},{240... | collective-permute-start | bytes 1228808 | tf_op jit(solution)/shard_map/cond/branch_3_fun/ppermute | solution.py:56
  151.9 20.4 %collective-permute-start.15 = (bf16[160,1280]{1,0:T(8,128)(2,1)S(1)}, bf16[160,1280]{1,0:T(8,128)(2,1)S(1)}, u32[]{:S(2)}, u32[]{:S(2)}) collective-permute-start(bf16[160,1280]{1,0:T(8,128)(2,1)S(1)} %get-tuple-element.122.refs_0_), channel_id=1, source_target_pairs={{128,0},{144,16},{160,32},{176,48},{192,64},{208,80},{224,96},{240... | collective-permute-start | bytes 1228808 | tf_op jit(solution)/shard_map/cond/branch_3_fun/ppermute | solution.py:56
  155.0 20.1 %collective-permute-start.16 = (bf16[160,1280]{1,0:T(8,128)(2,1)S(1)}, bf16[160,1280]{1,0:T(8,128)(2,1)S(1)}, u32[]{:S(2)}, u32[]{:S(2)}) collective-permute-start(bf16[160,1280]{1,0:T(8,128)(2,1)S(1)} %get-tuple-element.126), channel_id=1, source_target_pairs={{0,8},{1,9},{2,10},{3,11},{4,12},{5,13},{6,14},{7,15},{8,0},{9,1},... | collective-permute-start | bytes 1228808 | tf_op jit(solution)/shard_map/cond/branch_3_fun/ppermute | solution.py:40
  167.3 17.5 %collective-permute-start.19 = (bf16[160,1280]{1,0:T(8,128)(2,1)S(1)}, bf16[160,1280]{1,0:T(8,128)(2,1)S(1)}, u32[]{:S(2)}, u32[]{:S(2)}) collective-permute-start(bf16[160,1280]{1,0:T(8,128)(2,1)S(1)} %get-tuple-element.132.refs_6_.refs_0_), channel_id=1, source_target_pairs={{240,0},{0,16},{16,32},{32,48},{48,64},{64,80},{80,96},{96,112},{1... | collective-permute-start | bytes 1228808 | tf_op jit(solution)/shard_map/cond/branch_3_fun/ppermute | solution.py:56
  176.0 18.1 %copy-start.15 = (f32[160,2560]{1,0:T(8,128)}, f32[160,2560]{1,0:T(8,128)S(1)}, u32[]{:S(2)}) copy-start(f32[160,2560]{1,0:T(8,128)S(1)} %get-tuple-element.135) | copy-start | bytes 4915204 | tf_op jit(solution)/shard_map/cond
  176.0 17.9 %collective-permute-start.18 = (bf16[160,1280]{1,0:T(8,128)(2,1)S(1)}, bf16[160,1280]{1,0:T(8,128)(2,1)S(1)}, u32[]{:S(2)}, u32[]{:S(2)}) collective-permute-start(bf16[160,1280]{1,0:T(8,128)(2,1)S(1)} %get-tuple-element.134.refs_2_.refs_0_), channel_id=1, source_target_pairs={{240,0},{0,16},{16,32},{32,48},{48,64},{64,80},{80,96},{96,112},{1... | collective-permute-start | bytes 1228808 | tf_op jit(solution)/shard_map/cond/branch_3_fun/ppermute | solution.py:56
  194.1 0.9 copy-start.22
where the time goes:
time: 198 us; the launch traced here: 195 us
  waiting for transfers between devices  97 us (49%)
  starting transfers between devices  45.4 us (23%)
  Pallas kernels  44.6 us (23%)
  local copies, waits for them, and re-layouts  6.07 us (3%)
    ppermute x19, waiting for transfers between devices, fsdp_move(): return lax.ppermute(block, 'fsdp', [(i, target(i)) for i in range(N_FSDP)])  69.2 us
    ppermute x19, starting transfers between devices, fsdp_move(): return lax.ppermute(block, 'fsdp', [(i, target(i)) for i in range(N_FSDP)])  41.6 us
    ppermute x4, waiting for transfers between devices, group_move(): lax.ppermute(block, 'group', [((i - distance) % N_GROUP, i) for i in rang...  27.8 us
    pallas_call x6, Pallas kernels, products(): pl.pallas_call(partial(products_kernel, adds, layout, len(terms), tiles),...  26.7 us
    pallas_call x10, Pallas kernels, by_columns(): pl.pallas_call(body, grid=(width // TILE,), in_specs=[spec(*i) for i in i...  10.4 us
    pallas_call x2, Pallas kernels, turn(): pl.pallas_call(turn_kernel, grid_spec=pltpu.PrefetchScalarGridSpec(num_sc...  7.55 us
    unnamed x34, local copies, waits for them, and re-layouts  5.09 us
  transfers between devices with their start and end apart: 23, of which 15 were waited for; matrix products, arithmetic and copies ran while one was open for 0% of the time, Pallas kernels for 20%

commit v1 on v0

--- a/solution.py
+++ b/solution.py
@@ -177,10 +177,12 @@
 
 def strips(work):
     def one(i, carry):
-        work(pl.ds(pl.multiple_of(i * STRIP, STRIP), STRIP))
+        row = pl.multiple_of((i // 2) * STRIP, STRIP)
+        column = pl.multiple_of((i % 2) * (TILE // 2), TILE // 2)
+        work((pl.ds(row, STRIP), pl.ds(column, TILE // 2)))
         return carry
 
-    lax.fori_loop(0, ROWS // STRIP, one, 0)
+    lax.fori_loop(0, 2 * (ROWS // STRIP), one, 0)
 
 
 def by_columns(kernel, ins, outs, width, after=(), into=None):
@@ -336,8 +338,8 @@
     sums_b = across(b, near_b)
     state_a = first_step(a, *sums_a)
     near_d = near(1, b, far_cd)
+    state_b = first_step(b, *sums_b)
     total_c, give_c = across(a, near_c)
-    state_b = first_step(b, *sums_b)
     total_d, give_d = across(b, near_d)
     return lax.switch(
         step_index[0] % LEVELS,

time: 198 us -> 190 us (0.960); the launches traced: 195 us -> 190 us
  local copies, waits for them, and re-layouts: 6.07 us -> 3.14 us
  starting transfers between devices: 45.4 us -> 43.2 us
    ppermute x19, waiting for transfers between devices: 69.2 us -> 64.6 us  [fsdp_move(): return lax.ppermute(block, 'fsdp', [(i, target(i)) for i in range(N_FSDP)])]
    unnamed x34 -> x28, local copies, waits for them, and re-layouts: 5.09 us -> 2.17 us
    ppermute x4, waiting for transfers between devices: 27.8 us -> 30.6 us  [group_move(): lax.ppermute(block, 'group', [((i - distance) % N_GROUP, i) for i in rang...]
  transfers between devices with their start and end apart: 23 -> 23, of which waited for: 15 -> 14; matrix products, arithmetic and copies ran while one was open for 0% -> 0% of each run, Pallas kernels for 20% -> 21%
where the time goes in v1:
time: 190 us
  waiting for transfers between devices  95.3 us (50%)
  Pallas kernels  46 us (24%)
  starting transfers between devices  43.2 us (23%)
  local copies, waits for them, and re-layouts  3.14 us (2%)
    ppermute x19, waiting for transfers between devices, fsdp_move(): return lax.ppermute(block, 'fsdp', [(i, target(i)) for i in range(N_FSDP)])  64.6 us
    ppermute x19, starting transfers between devices, fsdp_move(): return lax.ppermute(block, 'fsdp', [(i, target(i)) for i in range(N_FSDP)])  39.9 us
    ppermute x4, waiting for transfers between devices, group_move(): lax.ppermute(block, 'group', [((i - distance) % N_GROUP, i) for i in rang...  30.6 us
    pallas_call x6, Pallas kernels, products(): pl.pallas_call(partial(products_kernel, adds, layout, len(terms), tiles),...  26.4 us
    pallas_call x10, Pallas kernels, by_columns(): pl.pallas_call(body, grid=(width // TILE,), in_specs=[spec(*i) for i in i...  12 us
    pallas_call x2, Pallas kernels, turn(): pl.pallas_call(turn_kernel, grid_spec=pltpu.PrefetchScalarGridSpec(num_sc...  7.55 us
  transfers between devices with their start and end apart: 23, of which 14 were waited for; matrix products, arithmetic and copies ran while one was open for 0% of the time, Pallas kernels for 21%

profile of v1, /device:TPU:68, one launch (start us, length us, event | category | flops | bytes accessed | tf_op | source)
XLA Modules:
  0.0 189.6 jit_solution(8626603655710403344)
XLA Ops:
  0.7 3.8 %shard_map.85 = (bf16[8,160,384]{2,1,0:T(8,128)(2,1)S(1)}, bf16[8,160,384]{2,1,0:T(8,128)(2,1)}) custom-call(s32[1]{0:T(128)} %bitcast.15.core_ref, bf16[2,1,384,2560]{3,2,1,0:T(8,128)(2,1)} %x_ref.3), custom_call_target="tpu_custom_call" | custom-call | flops 1024 | bytes 1024 | tf_op jit(solution)/shard_map/pallas_call | solution.py:83
  4.5 0.5 collective-permute-start.20
  5.0 3.8 %shard_map.86 = (bf16[8,160,384]{2,1,0:T(8,128)(2,1)S(1)}, bf16[8,160,384]{2,1,0:T(8,128)(2,1)}) custom-call(s32[1]{0:T(128)} %bitcast.15.core_ref, bf16[2,1,384,2560]{3,2,1,0:T(8,128)(2,1)} %x_ref.3, bf16[8,160,384]{2,1,0:T(8,128)(2,1)S(1)} %get-tuple-element.176.refs_0_.refs_1_.refs_2_.refs_3_.refs_4_.refs_5_), custom_call_target="tpu_custom_call" | custom-call | flops 1024 | bytes 1024 | tf_op jit(solution)/shard_map/pallas_call | solution.py:83
  9.1 5.2 %shard_map.87 = (bf16[1,160,2560]{2,1,0:T(8,128)(2,1)}, bf16[1,160,2560]{2,1,0:T(8,128)(2,1)}) custom-call(s32[2]{0:T(128)S(1)} %pad_add_fusion.blocks_ref, bf16[8,160,384]{2,1,0:T(8,128)(2,1)S(1)} %get-tuple-element.176.refs_0_.refs_1_.refs_2_.refs_3_.refs_4_.refs_5_, ...), custom_call_target="tpu_custom_call" | custom-call | flops 1024 | bytes 1024 | tf_op jit(solution)/shard_map/pallas_call | solution.py:153
  14.3 1.6 collective-permute-start.22
  15.9 1.6 collective-permute-start.23
  17.6 18.6 %collective-permute-done.22.refs_14_ = bf16[1,160,2560]{2,1,0:T(8,128)(2,1)} collective-permute-done((bf16[1,160,2560]{2,1,0:T(8,128)(2,1)}, bf16[1,160,2560]{2,1,0:T(8,128)(2,1)}, u32[]{:S(2)}, u32[]{:S(2)}) %collective-permute-start.22) | collective-permute-done | bytes 819232 | tf_op jit(solution)/shard_map/ppermute | solution.py:40
  36.2 2.1 %copy-done = bf16[2,1,384,2560]{3,2,1,0:T(8,128)(2,1)S(1)} copy-done((bf16[2,1,384,2560]{3,2,1,0:T(8,128)(2,1)S(1)}, bf16[2,1,384,2560]{3,2,1,0:T(8,128)(2,1)}, u32[]{:S(2)}) %copy-start) | copy-done | bytes 3932184
  38.4 4.3 %shard_map.88 = (bf16[2,160,1280]{2,1,0:T(8,128)(2,1)S(1)}, bf16[2,160,1280]{2,1,0:T(8,128)(2,1)S(1)}, bf16[1,160,1280]{2,1,0:T(8,128)(2,1)S(1)}, bf16[1,160,1280]{2,1,0:T(8,128)(2,1)S(1)}) custom-call(s32[6]{0:T(128)S(1)} %stack.26.blocks_ref, bf16[8,160,384]{2,1,0:T(8,128)(2,1)S(1)} %get-tuple-element.176.refs_0_.refs_1_.refs_2_.refs_3_.refs_4_.refs_5_, ...), custom_call_target="tpu_custom_call" | custom-call | flops 1024 | bytes 1024 | tf_op jit(solution)/shard_map/pallas_call | solution.py:153
  42.7 1.6 collective-permute-start.24
  44.3 1.7 collective-permute-start.25
  46.0 3.6 %shard_map.89 = (bf16[1,160,2560]{2,1,0:T(8,128)(2,1)S(1)}, bf16[1,160,2560]{2,1,0:T(8,128)(2,1)S(1)}) custom-call(s32[2]{0:T(128)S(1)} %pad_add_fusion.blocks_ref, bf16[8,160,384]{2,1,0:T(8,128)(2,1)S(1)} %get-tuple-element.178.refs_8_.refs_0_.refs_1_.refs_2_.refs_3_.refs_4_.refs_5_, ...), custom_call_target="tpu_custom_call" | custom-call | flops 1024 | bytes 1024 | tf_op jit(solution)/shard_map/pallas_call | solution.py:153
  49.6 0.4 collective-permute-start.29
  50.1 2.9 %collective-permute-start.30 = (bf16[1,160,2560]{2,1,0:T(8,128)(2,1)S(1)}, bf16[1,160,2560]{2,1,0:T(8,128)(2,1)S(1)}, u32[]{:S(2)}, u32[]{:S(2)}) collective-permute-start(bf16[1,160,2560]{2,1,0:T(8,128)(2,1)S(1)} %get-tuple-element.192), channel_id=1, source_target_pairs={{0,6},{1,7},{2,0},{3,1},{4,2},{5,3},{6,4},{7,5},{8,14},{9,15},{10,... | collective-permute-start | bytes 2457608 | tf_op jit(solution)/shard_map/ppermute | solution.py:40
  53.0 12.2 %collective-permute-done.24.refs_1_.refs_4_ = bf16[2,160,1280]{2,1,0:T(8,128)(2,1)S(1)} collective-permute-done((bf16[2,160,1280]{2,1,0:T(8,128)(2,1)S(1)}, bf16[2,160,1280]{2,1,0:T(8,128)(2,1)S(1)}, u32[]{:S(2)}, u32[]{:S(2)}) %collective-permute-start.24) | collective-permute-done | bytes 819232 | tf_op jit(solution)/shard_map/ppermute | solution.py:40
  65.5 0.5 shard_map.90
  66.0 4.1 %shard_map.91 = (bf16[2,160,1280]{2,1,0:T(8,128)(2,1)S(1)}, bf16[2,160,1280]{2,1,0:T(8,128)(2,1)S(1)}, bf16[1,160,1280]{2,1,0:T(8,128)(2,1)S(1)}, bf16[1,160,1280]{2,1,0:T(8,128)(2,1)S(1)}) custom-call(s32[6]{0:T(128)S(1)} %stack.26.blocks_ref, bf16[8,160,384]{2,1,0:T(8,128)(2,1)S(1)} %get-tuple-element.176.refs_0_.refs_1_.refs_2_.refs_3_.refs_4_.refs_5_, ...), custom_call_target="tpu_custom_call" | custom-call | flops 1024 | bytes 1024 | tf_op jit(solution)/shard_map/pallas_call | solution.py:153
  70.1 1.6 collective-permute-start.27
  71.7 1.9 %collective-permute-start.28 = (bf16[2,160,1280]{2,1,0:T(8,128)(2,1)S(1)}, bf16[2,160,1280]{2,1,0:T(8,128)(2,1)S(1)}, u32[]{:S(2)}, u32[]{:S(2)}) collective-permute-start(bf16[2,160,1280]{2,1,0:T(8,128)(2,1)S(1)} %get-tuple-element.190), channel_id=1, source_target_pairs={{0,6},{1,7},{2,0},{3,1},{4,2},{5,3},{6,4},{7,5},{8,14},{9,15},{10,... | collective-permute-start | bytes 2457608 | tf_op jit(solution)/shard_map/ppermute | solution.py:40
  73.6 5.4 %collective-permute-start.32 = (bf16[160,1280]{1,0:T(8,128)(2,1)S(1)}, bf16[160,1280]{1,0:T(8,128)(2,1)S(1)}, u32[]{:S(2)}, u32[]{:S(2)}) collective-permute-start(bf16[160,1280]{1,0:T(8,128)(2,1)S(1)} %get-tuple-element.196), channel_id=1, source_target_pairs={{0,8},{1,9},{2,10},{3,11},{4,12},{5,13},{6,14},{7,15},{8,0},{9,1},... | collective-permute-start | bytes 1228808 | tf_op jit(solution)/shard_map/ppermute | solution.py:40
  79.0 3.7 %collective-permute-done.29.refs_14_ = bf16[1,160,2560]{2,1,0:T(8,128)(2,1)S(1)} collective-permute-done((bf16[1,160,2560]{2,1,0:T(8,128)(2,1)S(1)}, bf16[1,160,2560]{2,1,0:T(8,128)(2,1)S(1)}, u32[]{:S(2)}, u32[]{:S(2)}) %collective-permute-start.29) | collective-permute-done | bytes 819232 | tf_op jit(solution)/shard_map/ppermute | solution.py:40
  83.0 4.2 %shard_map.92 = (bf16[2,160,1280]{2,1,0:T(8,128)(2,1)S(1)}, bf16[2,160,1280]{2,1,0:T(8,128)(2,1)S(1)}, bf16[1,160,1280]{2,1,0:T(8,128)(2,1)S(1)}, bf16[1,160,1280]{2,1,0:T(8,128)(2,1)S(1)}) custom-call(s32[6]{0:T(128)S(1)} %stack.26.blocks_ref, bf16[8,160,384]{2,1,0:T(8,128)(2,1)S(1)} %get-tuple-element.178.refs_8_.refs_0_.refs_1_.refs_2_.refs_3_.refs_4_.refs_5_, ...), custom_call_target="tpu_custom_call" | custom-call | flops 1024 | bytes 1024 | tf_op jit(solution)/shard_map/pallas_call | solution.py:153
  87.2 1.4 collective-permute-start.35
  88.6 1.9 %collective-permute-start.36 = (bf16[2,160,1280]{2,1,0:T(8,128)(2,1)S(1)}, bf16[2,160,1280]{2,1,0:T(8,128)(2,1)S(1)}, u32[]{:S(2)}, u32[]{:S(2)}) collective-permute-start(bf16[2,160,1280]{2,1,0:T(8,128)(2,1)S(1)} %get-tuple-element.204), channel_id=1, source_target_pairs={{0,6},{1,7},{2,0},{3,1},{4,2},{5,3},{6,4},{7,5},{8,14},{9,15},{10,... | collective-permute-start | bytes 2457608 | tf_op jit(solution)/shard_map/ppermute | solution.py:40
  90.6 9.7 %collective-permute-done.27.refs_1_.refs_4_ = bf16[2,160,1280]{2,1,0:T(8,128)(2,1)S(1)} collective-permute-done((bf16[2,160,1280]{2,1,0:T(8,128)(2,1)S(1)}, bf16[2,160,1280]{2,1,0:T(8,128)(2,1)S(1)}, u32[]{:S(2)}, u32[]{:S(2)}) %collective-permute-start.27) | collective-permute-done | bytes 819232 | tf_op jit(solution)/shard_map/ppermute | solution.py:40
  100.6 0.5 shard_map.93
  101.2 5.5 %collective-permute-start.31 = (bf16[160,1280]{1,0:T(8,128)(2,1)S(1)}, bf16[160,1280]{1,0:T(8,128)(2,1)S(1)}, u32[]{:S(2)}, u32[]{:S(2)}) collective-permute-start(bf16[160,1280]{1,0:T(8,128)(2,1)S(1)} %get-tuple-element.195), channel_id=1, source_target_pairs={{0,8},{1,9},{2,10},{3,11},{4,12},{5,13},{6,14},{7,15},{8,0},{9,1},... | collective-permute-start | bytes 1228808 | tf_op jit(solution)/shard_map/ppermute | solution.py:40
  106.7 2.2 %shard_map.94 = (f32[160,1280]{1,0:T(8,128)S(1)}, f32[160,1280]{1,0:T(8,128)}, bf16[160,1280]{1,0:T(8,128)(2,1)}) custom-call(bf16[1,160,2560]{2,1,0:T(8,128)(2,1)S(1)} %copy-done.2, bf16[1,160,2560]{2,1,0:T(8,128)(2,1)S(1)} %copy-done.3, bf16[1,160,2560]{2,1,0:T(8,128)(2,1)S(1)} %copy-done.4, f32[160,1280]{1,0:T(8,128)S(1)} %get-tuple-element.187.refs_16_.refs_3_, ...), custom_call_target="tpu_custom_call" | custom-call | flops 1024 | bytes 1024 | tf_op jit(solution)/shard_map/pallas_call | solution.py:206
  108.9 5.0 %shard_map.95 = (bf16[2,160,1280]{2,1,0:T(8,128)(2,1)S(1)}, bf16[2,160,1280]{2,1,0:T(8,128)(2,1)}, bf16[1,160,1280]{2,1,0:T(8,128)(2,1)S(1)}, bf16[1,160,1280]{2,1,0:T(8,128)(2,1)S(1)}) custom-call(s32[6]{0:T(128)S(1)} %stack.26.blocks_ref, bf16[8,160,384]{2,1,0:T(8,128)(2,1)S(1)} %get-tuple-element.178.refs_8_.refs_0_.refs_1_.refs_2_.refs_3_.refs_4_.refs_5_, ...), custom_call_target="tpu_custom_call" | custom-call | flops 1024 | bytes 1024 | tf_op jit(solution)/shard_map/pallas_call | solution.py:153
  113.9 1.3 collective-permute-start.33
  115.2 1.9 %collective-permute-start.34 = (bf16[2,160,1280]{2,1,0:T(8,128)(2,1)}, bf16[2,160,1280]{2,1,0:T(8,128)(2,1)S(1)}, u32[]{:S(2)}, u32[]{:S(2)}) collective-permute-start(bf16[2,160,1280]{2,1,0:T(8,128)(2,1)} %get-tuple-element.201), channel_id=1, source_target_pairs={{0,6},{1,7},{2,0},{3,1},{4,2},{5,3},{6,4},{7,5},{8,14},{9,15},{10,... | collective-permute-start | bytes 2457608 | tf_op jit(solution)/shard_map/ppermute | solution.py:40
  117.1 4.8 %collective-permute-done.31.refs_4_ = bf16[160,1280]{1,0:T(8,128)(2,1)S(1)} collective-permute-done((bf16[160,1280]{1,0:T(8,128)(2,1)S(1)}, bf16[160,1280]{1,0:T(8,128)(2,1)S(1)}, u32[]{:S(2)}, u32[]{:S(2)}) %collective-permute-start.31) | collective-permute-done | bytes 409632 | tf_op jit(solution)/shard_map/ppermute | solution.py:40
  121.9 2.2 %shard_map.96 = (f32[160,1280]{1,0:T(8,128)S(1)}, f32[160,1280]{1,0:T(8,128)}, bf16[160,1280]{1,0:T(8,128)(2,1)}) custom-call(bf16[1,160,2560]{2,1,0:T(8,128)(2,1)S(1)} %copy-done.2, bf16[1,160,2560]{2,1,0:T(8,128)(2,1)S(1)} %copy-done.3, bf16[1,160,2560]{2,1,0:T(8,128)(2,1)S(1)} %copy-done.4, f32[160,1280]{1,0:T(8,128)S(1)} %get-tuple-element.194.refs_5_.refs_3_, ...), custom_call_target="tpu_custom_call" | custom-call | flops 1024 | bytes 1024 | tf_op jit(solution)/shard_map/pallas_call | solution.py:206
  124.2 1.6 shard_map.97
  125.8 5.2 %collective-permute-start.37 = (bf16[160,1280]{1,0:T(8,128)(2,1)}, bf16[160,1280]{1,0:T(8,128)(2,1)}, u32[]{:S(2)}, u32[]{:S(2)}) collective-permute-start(bf16[160,1280]{1,0:T(8,128)(2,1)} %get-tuple-element.211), channel_id=1, source_target_pairs={{0,8},{1,9},{2,10},{3,11},{4,12},{5,13},{6,14},{7,15},{8,0},{9,1},... | collective-permute-start | bytes 1228808 | tf_op jit(solution)/shard_map/ppermute | solution.py:40
  131.7 2.0 %collective-permute-done.33.refs_1_.refs_4_ = bf16[2,160,1280]{2,1,0:T(8,128)(2,1)S(1)} collective-permute-done((bf16[2,160,1280]{2,1,0:T(8,128)(2,1)S(1)}, bf16[2,160,1280]{2,1,0:T(8,128)(2,1)S(1)}, u32[]{:S(2)}, u32[]{:S(2)}) %collective-permute-start.33) | collective-permute-done | bytes 819232 | tf_op jit(solution)/shard_map/ppermute | solution.py:40
  133.8 0.6 shard_map.98
  134.4 12.3 %collective-permute-done.37 = bf16[160,1280]{1,0:T(8,128)(2,1)} collective-permute-done((bf16[160,1280]{1,0:T(8,128)(2,1)}, bf16[160,1280]{1,0:T(8,128)(2,1)}, u32[]{:S(2)}, u32[]{:S(2)}) %collective-permute-start.37) | collective-permute-done | bytes 409632 | tf_op jit(solution)/shard_map/ppermute | solution.py:40
  146.8 42.8 %conditional.1 = (bf16[1,160,2560]{2,1,0:T(8,128)(2,1)}, f32[1,160,2560]{2,1,0:T(8,128)}) conditional(s32[]{:T(128)} %clamp.3, (bf16[160,1280]{1,0:T(8,128)(2,1)S(1)}, bf16[160,1280]{1,0:T(8,128)(2,1)S(1)}, bf16[160,1280]{1,0:T(8,128)(2,1)S(1)}, f32[160,1280]{1,0:T(8,128)S(1)}, f32[160,1280]{1,0:T(8,128)S(1)}, ...), branch_computations={%region_0.1_spmd, %region_1.2_spmd, %region_2.3_spmd, %region_3.4_... | conditional | flops 4096 | bytes 18026768 | solution.py:344
  147.0 1.3 collective-permute-start.12
  148.6 3.3 %collective-permute-start.11 = (bf16[160,1280]{1,0:T(8,128)(2,1)S(1)}, bf16[160,1280]{1,0:T(8,128)(2,1)S(1)}, u32[]{:S(2)}, u32[]{:S(2)}) collective-permute-start(bf16[160,1280]{1,0:T(8,128)(2,1)S(1)} %get-tuple-element.112), channel_id=1, source_target_pairs={{0,8},{1,9},{2,10},{3,11},{4,12},{5,13},{6,14},{7,15},{8,0},{9,1},... | collective-permute-start | bytes 1228808 | tf_op jit(solution)/shard_map/cond/branch_2_fun/ppermute | solution.py:40
  151.9 7.6 %collective-permute-done.12.refs_1_ = bf16[160,1280]{1,0:T(8,128)(2,1)S(1)} collective-permute-done((bf16[160,1280]{1,0:T(8,128)(2,1)S(1)}, bf16[160,1280]{1,0:T(8,128)(2,1)S(1)}, u32[]{:S(2)}, u32[]{:S(2)}) %collective-permute-start.12) | collective-permute-done | bytes 409632 | tf_op jit(solution)/shard_map/cond/branch_2_fun/ppermute | solution.py:56
  159.5 2.2 %branch_2_fun.4 = (bf16[160,1280]{1,0:T(8,128)(2,1)S(1)}, f32[160,2560]{1,0:T(8,128)S(1)}) custom-call(bf16[160,1280]{1,0:T(8,128)(2,1)S(1)} %get-tuple-element.113.refs_0_, bf16[160,1280]{1,0:T(8,128)(2,1)S(1)} %collective-permute-done.12.refs_1_, f32[160,1280]{1,0:T(8,128)S(1)} %get-tuple-element.114.refs_2_, f32[160,1280]{1,0:T(8,128)S(1)} %get-tuple-element.115.refs_3_, ...), custom_call_target="tpu_custom_call" | custom-call | flops 1024 | bytes 1024 | tf_op jit(solution)/shard_map/cond/branch_2_fun/pallas_call | solution.py:206
  161.7 1.7 collective-permute-start.14
  163.4 14.1 %collective-permute-done.10.refs_1_ = bf16[160,1280]{1,0:T(8,128)(2,1)S(1)} collective-permute-done((bf16[160,1280]{1,0:T(8,128)(2,1)S(1)}, bf16[160,1280]{1,0:T(8,128)(2,1)S(1)}, u32[]{:S(2)}, u32[]{:S(2)}) %collective-permute-start.10) | collective-permute-done | bytes 409632 | tf_op jit(solution)/shard_map/cond/branch_2_fun/ppermute | solution.py:56
  177.5 1.2 branch_2_fun.5
  179.2 9.0 %collective-permute-done.13.refs_1_ = bf16[160,1280]{1,0:T(8,128)(2,1)S(1)} collective-permute-done((bf16[160,1280]{1,0:T(8,128)(2,1)S(1)}, bf16[160,1280]{1,0:T(8,128)(2,1)S(1)}, u32[]{:S(2)}, u32[]{:S(2)}) %collective-permute-start.13) | collective-permute-done | bytes 409632 | tf_op jit(solution)/shard_map/cond/branch_2_fun/ppermute | solution.py:56
  188.7 0.9 copy-done.14
  (51 shorter events, 2.8 us)
Async XLA Ops:
  0.6 8.5 %collective-permute-start.21 = (bf16[2,1,384,2560]{3,2,1,0:T(8,128)(2,1)}, bf16[2,1,384,2560]{3,2,1,0:T(8,128)(2,1)}, u32[]{:S(2)}, u32[]{:S(2)}) collective-permute-start(bf16[2,1,384,2560]{3,2,1,0:T(8,128)(2,1)} %refs_12_.7), channel_id=1, source_target_pairs={{0,1},{1,0},{2,3},{3,2},{4,5},{5,4},{6,7},{7,6},{8,9},{9,8},{10,11... | collective-permute-start | bytes 11796488 | tf_op jit(solution)/shard_map/ppermute | solution.py:40
  4.5 4.6 %collective-permute-start.20 = (bf16[8,160,384]{2,1,0:T(8,128)(2,1)}, bf16[8,160,384]{2,1,0:T(8,128)(2,1)S(1)}, u32[]{:S(2)}, u32[]{:S(2)}) collective-permute-start(bf16[8,160,384]{2,1,0:T(8,128)(2,1)} %get-tuple-element.177), channel_id=1, source_target_pairs={{0,1},{1,0},{2,3},{3,2},{4,5},{5,4},{6,7},{7,6},{8,9},{9,8},{10,11... | collective-permute-start | bytes 2949128 | tf_op jit(solution)/shard_map/ppermute | solution.py:40
  14.3 21.9 %collective-permute-start.22 = (bf16[1,160,2560]{2,1,0:T(8,128)(2,1)}, bf16[1,160,2560]{2,1,0:T(8,128)(2,1)}, u32[]{:S(2)}, u32[]{:S(2)}) collective-permute-start(bf16[1,160,2560]{2,1,0:T(8,128)(2,1)} %get-tuple-element.179.refs_16_), channel_id=1, source_target_pairs={{0,2},{1,3},{2,4},{3,5},{4,6},{5,7},{6,0},{7,1},{8,10},{9,11},{10,... | collective-permute-start | bytes 2457608 | tf_op jit(solution)/shard_map/ppermute | solution.py:40
  15.9 20.3 %collective-permute-start.23 = (bf16[1,160,2560]{2,1,0:T(8,128)(2,1)}, bf16[1,160,2560]{2,1,0:T(8,128)(2,1)}, u32[]{:S(2)}, u32[]{:S(2)}) collective-permute-start(bf16[1,160,2560]{2,1,0:T(8,128)(2,1)} %get-tuple-element.180), channel_id=1, source_target_pairs={{0,6},{1,7},{2,0},{3,1},{4,2},{5,3},{6,4},{7,5},{8,14},{9,15},{10,... | collective-permute-start | bytes 2457608 | tf_op jit(solution)/shard_map/ppermute | solution.py:40
  17.5 28.5 %collective-permute-start.26 = (bf16[8,160,384]{2,1,0:T(8,128)(2,1)}, bf16[8,160,384]{2,1,0:T(8,128)(2,1)}, u32[]{:S(2)}, u32[]{:S(2)}) collective-permute-start(bf16[8,160,384]{2,1,0:T(8,128)(2,1)} %get-tuple-element.185), channel_id=1, source_target_pairs={{0,1},{1,0},{2,3},{3,2},{4,5},{5,4},{6,7},{7,6},{8,9},{9,8},{10,11... | collective-permute-start | bytes 2949128 | tf_op jit(solution)/shard_map/ppermute | solution.py:40
  36.2 2.1 %copy-start = (bf16[2,1,384,2560]{3,2,1,0:T(8,128)(2,1)S(1)}, bf16[2,1,384,2560]{3,2,1,0:T(8,128)(2,1)}, u32[]{:S(2)}) copy-start(bf16[2,1,384,2560]{3,2,1,0:T(8,128)(2,1)} %refs_12_.7) | copy-start | bytes 11796484
  38.4 7.7 %copy-start.1 = (bf16[2,1,384,2560]{3,2,1,0:T(8,128)(2,1)S(1)}, bf16[2,1,384,2560]{3,2,1,0:T(8,128)(2,1)}, u32[]{:S(2)}) copy-start(bf16[2,1,384,2560]{3,2,1,0:T(8,128)(2,1)} %refs_12_.7) | copy-start | bytes 11796484
  42.7 22.5 %collective-permute-start.24 = (bf16[2,160,1280]{2,1,0:T(8,128)(2,1)S(1)}, bf16[2,160,1280]{2,1,0:T(8,128)(2,1)S(1)}, u32[]{:S(2)}, u32[]{:S(2)}) collective-permute-start(bf16[2,160,1280]{2,1,0:T(8,128)(2,1)S(1)} %get-tuple-element.182.refs_8_), channel_id=1, source_target_pairs={{0,2},{1,3},{2,4},{3,5},{4,6},{5,7},{6,0},{7,1},{8,10},{9,11},{10,... | collective-permute-start | bytes 2457608 | tf_op jit(solution)/shard_map/ppermute | solution.py:40
  44.3 21.2 %collective-permute-start.25 = (bf16[2,160,1280]{2,1,0:T(8,128)(2,1)S(1)}, bf16[2,160,1280]{2,1,0:T(8,128)(2,1)S(1)}, u32[]{:S(2)}, u32[]{:S(2)}) collective-permute-start(bf16[2,160,1280]{2,1,0:T(8,128)(2,1)S(1)} %get-tuple-element.183), channel_id=1, source_target_pairs={{0,6},{1,7},{2,0},{3,1},{4,2},{5,3},{6,4},{7,5},{8,14},{9,15},{10,... | collective-permute-start | bytes 2457608 | tf_op jit(solution)/shard_map/ppermute | solution.py:40
  49.6 33.1 %collective-permute-start.29 = (bf16[1,160,2560]{2,1,0:T(8,128)(2,1)S(1)}, bf16[1,160,2560]{2,1,0:T(8,128)(2,1)S(1)}, u32[]{:S(2)}, u32[]{:S(2)}) collective-permute-start(bf16[1,160,2560]{2,1,0:T(8,128)(2,1)S(1)} %get-tuple-element.186.refs_6_), channel_id=1, source_target_pairs={{0,2},{1,3},{2,4},{3,5},{4,6},{5,7},{6,0},{7,1},{8,10},{9,11},{10,... | collective-permute-start | bytes 2457608 | tf_op jit(solution)/shard_map/ppermute | solution.py:40
  50.1 33.0 %collective-permute-start.30 = (bf16[1,160,2560]{2,1,0:T(8,128)(2,1)S(1)}, bf16[1,160,2560]{2,1,0:T(8,128)(2,1)S(1)}, u32[]{:S(2)}, u32[]{:S(2)}) collective-permute-start(bf16[1,160,2560]{2,1,0:T(8,128)(2,1)S(1)} %get-tuple-element.192), channel_id=1, source_target_pairs={{0,6},{1,7},{2,0},{3,1},{4,2},{5,3},{6,4},{7,5},{8,14},{9,15},{10,... | collective-permute-start | bytes 2457608 | tf_op jit(solution)/shard_map/ppermute | solution.py:40
  70.1 30.2 %collective-permute-start.27 = (bf16[2,160,1280]{2,1,0:T(8,128)(2,1)S(1)}, bf16[2,160,1280]{2,1,0:T(8,128)(2,1)S(1)}, u32[]{:S(2)}, u32[]{:S(2)}) collective-permute-start(bf16[2,160,1280]{2,1,0:T(8,128)(2,1)S(1)} %get-tuple-element.189.refs_16_), channel_id=1, source_target_pairs={{0,2},{1,3},{2,4},{3,5},{4,6},{5,7},{6,0},{7,1},{8,10},{9,11},{10,... | collective-permute-start | bytes 2457608 | tf_op jit(solution)/shard_map/ppermute | solution.py:40
  71.7 28.9 %collective-permute-start.28 = (bf16[2,160,1280]{2,1,0:T(8,128)(2,1)S(1)}, bf16[2,160,1280]{2,1,0:T(8,128)(2,1)S(1)}, u32[]{:S(2)}, u32[]{:S(2)}) collective-permute-start(bf16[2,160,1280]{2,1,0:T(8,128)(2,1)S(1)} %get-tuple-element.190), channel_id=1, source_target_pairs={{0,6},{1,7},{2,0},{3,1},{4,2},{5,3},{6,4},{7,5},{8,14},{9,15},{10,... | collective-permute-start | bytes 2457608 | tf_op jit(solution)/shard_map/ppermute | solution.py:40
  73.6 33.0 %collective-permute-start.32 = (bf16[160,1280]{1,0:T(8,128)(2,1)S(1)}, bf16[160,1280]{1,0:T(8,128)(2,1)S(1)}, u32[]{:S(2)}, u32[]{:S(2)}) collective-permute-start(bf16[160,1280]{1,0:T(8,128)(2,1)S(1)} %get-tuple-element.196), channel_id=1, source_target_pairs={{0,8},{1,9},{2,10},{3,11},{4,12},{5,13},{6,14},{7,15},{8,0},{9,1},... | collective-permute-start | bytes 1228808 | tf_op jit(solution)/shard_map/ppermute | solution.py:40
  87.2 36.9 %collective-permute-start.35 = (bf16[2,160,1280]{2,1,0:T(8,128)(2,1)S(1)}, bf16[2,160,1280]{2,1,0:T(8,128)(2,1)S(1)}, u32[]{:S(2)}, u32[]{:S(2)}) collective-permute-start(bf16[2,160,1280]{2,1,0:T(8,128)(2,1)S(1)} %get-tuple-element.193.refs_6_), channel_id=1, source_target_pairs={{0,2},{1,3},{2,4},{3,5},{4,6},{5,7},{6,0},{7,1},{8,10},{9,11},{10,... | collective-permute-start | bytes 2457608 | tf_op jit(solution)/shard_map/ppermute | solution.py:40
  88.6 35.5 %collective-permute-start.36 = (bf16[2,160,1280]{2,1,0:T(8,128)(2,1)S(1)}, bf16[2,160,1280]{2,1,0:T(8,128)(2,1)S(1)}, u32[]{:S(2)}, u32[]{:S(2)}) collective-permute-start(bf16[2,160,1280]{2,1,0:T(8,128)(2,1)S(1)} %get-tuple-element.204), channel_id=1, source_target_pairs={{0,6},{1,7},{2,0},{3,1},{4,2},{5,3},{6,4},{7,5},{8,14},{9,15},{10,... | collective-permute-start | bytes 2457608 | tf_op jit(solution)/shard_map/ppermute | solution.py:40
  100.6 6.0 %copy-start.2 = (bf16[1,160,2560]{2,1,0:T(8,128)(2,1)S(1)}, bf16[1,160,2560]{2,1,0:T(8,128)(2,1)}, u32[]{:S(2)}) copy-start(bf16[1,160,2560]{2,1,0:T(8,128)(2,1)} %refs_0_.3) | copy-start | bytes 2457604
  100.6 6.0 %copy-start.3 = (bf16[1,160,2560]{2,1,0:T(8,128)(2,1)S(1)}, bf16[1,160,2560]{2,1,0:T(8,128)(2,1)}, u32[]{:S(2)}) copy-start(bf16[1,160,2560]{2,1,0:T(8,128)(2,1)} %refs_1_.3) | copy-start | bytes 2457604
  100.6 6.0 %copy-start.4 = (bf16[1,160,2560]{2,1,0:T(8,128)(2,1)S(1)}, bf16[1,160,2560]{2,1,0:T(8,128)(2,1)}, u32[]{:S(2)}) copy-start(bf16[1,160,2560]{2,1,0:T(8,128)(2,1)} %refs_2_.3) | copy-start | bytes 2457604
  101.2 20.7 %collective-permute-start.31 = (bf16[160,1280]{1,0:T(8,128)(2,1)S(1)}, bf16[160,1280]{1,0:T(8,128)(2,1)S(1)}, u32[]{:S(2)}, u32[]{:S(2)}) collective-permute-start(bf16[160,1280]{1,0:T(8,128)(2,1)S(1)} %get-tuple-element.195), channel_id=1, source_target_pairs={{0,8},{1,9},{2,10},{3,11},{4,12},{5,13},{6,14},{7,15},{8,0},{9,1},... | collective-permute-start | bytes 1228808 | tf_op jit(solution)/shard_map/ppermute | solution.py:40
  108.9 5.0 %copy-start.10 = (f32[160,1280]{1,0:T(8,128)}, f32[160,1280]{1,0:T(8,128)S(1)}, u32[]{:S(2)}) copy-start(f32[160,1280]{1,0:T(8,128)S(1)} %get-tuple-element.197.refs_16_) | copy-start | bytes 2457604
  113.9 19.9 %collective-permute-start.33 = (bf16[2,160,1280]{2,1,0:T(8,128)(2,1)S(1)}, bf16[2,160,1280]{2,1,0:T(8,128)(2,1)S(1)}, u32[]{:S(2)}, u32[]{:S(2)}) collective-permute-start(bf16[2,160,1280]{2,1,0:T(8,128)(2,1)S(1)} %get-tuple-element.198.refs_5_), channel_id=1, source_target_pairs={{0,2},{1,3},{2,4},{3,5},{4,6},{5,7},{6,0},{7,1},{8,10},{9,11},{10,... | collective-permute-start | bytes 2457608 | tf_op jit(solution)/shard_map/ppermute | solution.py:40
  115.2 18.5 %collective-permute-start.34 = (bf16[2,160,1280]{2,1,0:T(8,128)(2,1)}, bf16[2,160,1280]{2,1,0:T(8,128)(2,1)S(1)}, u32[]{:S(2)}, u32[]{:S(2)}) collective-permute-start(bf16[2,160,1280]{2,1,0:T(8,128)(2,1)} %get-tuple-element.201), channel_id=1, source_target_pairs={{0,6},{1,7},{2,0},{3,1},{4,2},{5,3},{6,4},{7,5},{8,14},{9,15},{10,... | collective-permute-start | bytes 2457608 | tf_op jit(solution)/shard_map/ppermute | solution.py:40
  124.2 1.7 copy-start.16
  125.8 20.9 %collective-permute-start.37 = (bf16[160,1280]{1,0:T(8,128)(2,1)}, bf16[160,1280]{1,0:T(8,128)(2,1)}, u32[]{:S(2)}, u32[]{:S(2)}) collective-permute-start(bf16[160,1280]{1,0:T(8,128)(2,1)} %get-tuple-element.211), channel_id=1, source_target_pairs={{0,8},{1,9},{2,10},{3,11},{4,12},{5,13},{6,14},{7,15},{8,0},{9,1},... | collective-permute-start | bytes 1228808 | tf_op jit(solution)/shard_map/ppermute | solution.py:40
  133.8 13.0 %copy-start.9 = (f32[160,1280]{1,0:T(8,128)S(1)}, f32[160,1280]{1,0:T(8,128)}, u32[]{:S(2)}) copy-start(f32[160,1280]{1,0:T(8,128)} %get-tuple-element.207.refs_6_) | copy-start | bytes 2457604
  133.8 13.0 %copy-start.11 = (f32[160,1280]{1,0:T(8,128)S(1)}, f32[160,1280]{1,0:T(8,128)}, u32[]{:S(2)}) copy-start(f32[160,1280]{1,0:T(8,128)} %copy-done.10) | copy-start | bytes 2457604
  133.8 13.0 %copy-start.17 = (f32[160,1280]{1,0:T(8,128)S(1)}, f32[160,1280]{1,0:T(8,128)}, u32[]{:S(2)}) copy-start(f32[160,1280]{1,0:T(8,128)} %copy-done.16) | copy-start | bytes 2457604
  133.8 13.0 %copy-start.18 = (f32[160,1280]{1,0:T(8,128)S(1)}, f32[160,1280]{1,0:T(8,128)}, u32[]{:S(2)}) copy-start(f32[160,1280]{1,0:T(8,128)} %get-tuple-element.210) | copy-start | bytes 2457604
  133.8 13.0 %copy-start.19 = (f32[160,1280]{1,0:T(8,128)S(1)}, f32[160,1280]{1,0:T(8,128)}, u32[]{:S(2)}) copy-start(f32[160,1280]{1,0:T(8,128)} %get-tuple-element.212) | copy-start | bytes 2457604
  133.8 13.0 %copy-start.20 = (bf16[160,1280]{1,0:T(8,128)(2,1)S(1)}, bf16[160,1280]{1,0:T(8,128)(2,1)}, u32[]{:S(2)}) copy-start(bf16[160,1280]{1,0:T(8,128)(2,1)} %get-tuple-element.209) | copy-start | bytes 1228804
  133.8 13.0 %copy-start.21 = (bf16[160,1280]{1,0:T(8,128)(2,1)S(1)}, bf16[160,1280]{1,0:T(8,128)(2,1)}, u32[]{:S(2)}) copy-start(bf16[160,1280]{1,0:T(8,128)(2,1)} %get-tuple-element.199) | copy-start | bytes 1228804
  147.0 12.5 %collective-permute-start.12 = (bf16[160,1280]{1,0:T(8,128)(2,1)S(1)}, bf16[160,1280]{1,0:T(8,128)(2,1)S(1)}, u32[]{:S(2)}, u32[]{:S(2)}) collective-permute-start(bf16[160,1280]{1,0:T(8,128)(2,1)S(1)} %get-tuple-element.113.refs_0_), channel_id=1, source_target_pairs={{192,0},{208,16},{224,32},{240,48},{0,64},{16,80},{32,96},{48,112}... | collective-permute-start | bytes 1228808 | tf_op jit(solution)/shard_map/cond/branch_2_fun/ppermute | solution.py:56
  148.3 29.2 %collective-permute-start.10 = (bf16[160,1280]{1,0:T(8,128)(2,1)S(1)}, bf16[160,1280]{1,0:T(8,128)(2,1)S(1)}, u32[]{:S(2)}, u32[]{:S(2)}) collective-permute-start(bf16[160,1280]{1,0:T(8,128)(2,1)S(1)} %get-tuple-element.108.refs_0_), channel_id=1, source_target_pairs={{192,0},{208,16},{224,32},{240,48},{0,64},{16,80},{32,96},{48,112}... | collective-permute-start | bytes 1228808 | tf_op jit(solution)/shard_map/cond/branch_2_fun/ppermute | solution.py:56
  148.6 28.8 %collective-permute-start.11 = (bf16[160,1280]{1,0:T(8,128)(2,1)S(1)}, bf16[160,1280]{1,0:T(8,128)(2,1)S(1)}, u32[]{:S(2)}, u32[]{:S(2)}) collective-permute-start(bf16[160,1280]{1,0:T(8,128)(2,1)S(1)} %get-tuple-element.112), channel_id=1, source_target_pairs={{0,8},{1,9},{2,10},{3,11},{4,12},{5,13},{6,14},{7,15},{8,0},{9,1},... | collective-permute-start | bytes 1228808 | tf_op jit(solution)/shard_map/cond/branch_2_fun/ppermute | solution.py:40
  161.7 17.1 %collective-permute-start.14 = (bf16[160,1280]{1,0:T(8,128)(2,1)S(1)}, bf16[160,1280]{1,0:T(8,128)(2,1)S(1)}, u32[]{:S(2)}, u32[]{:S(2)}) collective-permute-start(bf16[160,1280]{1,0:T(8,128)(2,1)S(1)} %get-tuple-element.118.refs_6_.refs_0_), channel_id=1, source_target_pairs={{128,0},{144,16},{160,32},{176,48},{192,64},{208,80},{224,96},{240... | collective-permute-start | bytes 1228808 | tf_op jit(solution)/shard_map/cond/branch_2_fun/ppermute | solution.py:56
  178.7 10.0 %copy-start.7 = (f32[160,2560]{1,0:T(8,128)}, f32[160,2560]{1,0:T(8,128)S(1)}, u32[]{:S(2)}) copy-start(f32[160,2560]{1,0:T(8,128)S(1)} %get-tuple-element.121) | copy-start | bytes 4915204 | tf_op jit(solution)/shard_map/cond
  178.7 9.5 %collective-permute-start.13 = (bf16[160,1280]{1,0:T(8,128)(2,1)S(1)}, bf16[160,1280]{1,0:T(8,128)(2,1)S(1)}, u32[]{:S(2)}, u32[]{:S(2)}) collective-permute-start(bf16[160,1280]{1,0:T(8,128)(2,1)S(1)} %get-tuple-element.120.refs_2_.refs_0_), channel_id=1, source_target_pairs={{128,0},{144,16},{160,32},{176,48},{192,64},{208,80},{224,96},{240... | collective-permute-start | bytes 1228808 | tf_op jit(solution)/shard_map/cond/branch_2_fun/ppermute | solution.py:56
  188.7 0.9 copy-start.14
